TPU v7x, 32 devices: a whole 2x2x4 slice. The times are simulated.
32 devices in a mesh: ckpt: 2 (over x), fsdp: 8 (over z, y), dp: 2 (over core).
Axes of the slice: x: 2, y: 2, z: 4, core: 2. Of those that a mesh axis runs over, the one named last changes fastest.
Arguments:
- hidden_in: bfloat16 [8, 5120, 1024], P(('ckpt', 'dp'), 'fsdp'), parts along dimension 0, may hold values from -160 to 160, as said below
- cotangent: bfloat16 [8, 5120, 1024], P(('ckpt', 'dp'), 'fsdp'), parts along dimension 0, may hold values from -16 to 16
- context: bfloat16 [8, 2560, 1024], P(('ckpt', 'dp'), 'fsdp'), parts along dimension 0, may hold values from -6 to 6
- norm_gain: bfloat16 [5120], P('fsdp'), may hold values from 0.099609375 to 1.8984375
- signs_rows: int32 [8192], replicated, may hold values 0 or 1
- column_sign_flips: int32 [2048], replicated, may hold values 0 or 1
- kept_index: int32 [16384], replicated, may hold values from 0 to 16777215
Outputs:
- projections: float32 [8, 16384], P(('ckpt', 'dp'), 'fsdp'), parts along dimension 0
There are 2 independent parts, one for each index of `ckpt`. A program takes and returns all parts, laid end to end along the dimension named above; an argument that names none is the same for every part. Nothing has to cross between parts.
Inputs may be any that keep to these rules, and one draw needn't show every extreme that they name: `hidden_in`: each entry is a bfloat16 value of order one to some tens, with token scales that differ from token to token.
All inputs are finite; a program needn't handle non-finite values.
Results may differ from a plain program's by a relative error of at most 0.005.
Values may be sent and summed in bfloat16 or wider, within the bound.
A program may use at most 256 MiB of HBM per device.

v0:
```python
import math

import jax
import jax.numpy as jnp
from jax import lax
from jax.sharding import PartitionSpec as P

D = 5120
ROWS_A = 8192
COLS_B = 2048
SEQ = 1024


EPS = 1e-06


def bitwise_parity_value(values, bit_count):
    parity_flag = jnp.zeros_like(values)
    for shift_count in range(bit_count):
        parity_flag = parity_flag ^ values >> shift_count & 1
    return parity_flag


def hadamard(order):
    indices = jnp.arange(order, dtype=jnp.int32)
    parity_bits = bitwise_parity_value(indices[:, None] & indices[None, :], order.bit_length())
    return (1 - 2 * parity_bits).astype(jnp.float32)


def on_device(hidden_in, cotangent, context, norm_gain, signs_rows, column_sign_flips, kept_index):
    position_index = lax.axis_index("fsdp")
    hidden = hidden_in.astype(jnp.float32)
    weighted = norm_gain.astype(jnp.float32)[None, :, None] * cotangent.astype(jnp.float32)
    square_sum, cross_sum = lax.psum(
        (jnp.sum(hidden * hidden, axis=1), jnp.sum(weighted * hidden, axis=1)), "fsdp"
    )
    inverse = lax.rsqrt(square_sum / D + EPS)
    grad_hidden = (
        weighted * inverse[:, None, :] - hidden * (cross_sum * inverse**3 / D)[:, None, :]
    ).astype(jnp.bfloat16)
    blocks = []
    for micro in range(context.shape[0]):
        blocks.append(
            jnp.einsum(
                "ds,ns->dn",
                grad_hidden[micro],
                lax.all_gather(context[micro], "fsdp", axis=0, tiled=True),
                preferred_element_type=jnp.float32,
            )
        )
    gradient_matrix = jnp.stack(blocks, axis=0).astype(jnp.bfloat16)
    local_rows = gradient_matrix.shape[1] * gradient_matrix.shape[2] // COLS_B
    zero_padded_rows = gradient_matrix.reshape(gradient_matrix.shape[0], local_rows, COLS_B)
    sign_a = (1 - 2 * signs_rows).astype(jnp.float32)
    sign_b = (1 - 2 * column_sign_flips).astype(jnp.float32)
    sign_lookup_matrix = (sign_b[:, None] * hadamard(COLS_B)).astype(jnp.bfloat16)
    mixed_rows = jnp.einsum(
        "lws,sv->lwv", zero_padded_rows, sign_lookup_matrix, preferred_element_type=jnp.float32
    ).astype(jnp.bfloat16)
    kept_row = kept_index // COLS_B
    kept_col = kept_index % COLS_B
    scale = 1.0 / math.sqrt(ROWS_A * COLS_B * SEQ)
    row_index = position_index * local_rows + jnp.arange(local_rows, dtype=jnp.int32)
    local_signs = lax.dynamic_slice_in_dim(sign_a, position_index * local_rows, local_rows, 0)
    parity_bits = bitwise_parity_value(row_index[:, None] & kept_row[None, :], ROWS_A.bit_length())
    factor = (1 - 2 * parity_bits).astype(jnp.float32) * local_signs[:, None]
    picked = jnp.take(mixed_rows, kept_col, axis=2).astype(jnp.float32)
    partial_value = jnp.einsum("mrp,rp->mp", picked, factor, precision=lax.Precision.HIGHEST)
    return lax.psum_scatter(partial_value * scale, "fsdp", scatter_dimension=1, tiled=True)


def solution(mesh):
    return jax.shard_map(
        on_device,
        mesh=mesh,
        in_specs=(
            P(("ckpt", "dp"), "fsdp", None),
            P(("ckpt", "dp"), "fsdp", None),
            P(("ckpt", "dp"), "fsdp", None),
            P("fsdp"),
            P(),
            P(),
            P(),
        ),
        out_specs=P(("ckpt", "dp"), "fsdp"),
        check_vma=False,
    )
```

profile of v0, /device:TPU:0, one launch (start us, length us, event | category | flops | bytes accessed | tf_op | source)
XLA Modules:
  0.0 920.7 jit_solution(13686255179626228856)
XLA Ops:
  6.5 2.5 fusion.89
  9.1 0.7 all-gather.5.cloned.1.call-update
  9.8 0.9 broadcast_clamp_fusion
  10.7 0.8 fusion.75
  11.5 79.1 %fusion.30 = f32[16384,800]{0,1:T(8,128)} fusion(f32[800]{0:T(1024)S(1)} %get-tuple-element.15, s32[16384]{0:T(1024)S(1)} %get-tuple-element.12, s32[800]{0:T(1024)S(1)} %get-tuple-element.16), kind=kLoop, calls=%fused_computation.47 | loop fusion | flops 602931200 | bytes 52500736
  90.7 58.5 %copy.17 = f32[16384,800]{1,0:T(8,128)} copy(f32[16384,800]{0,1:T(8,128)} %fusion.30) | data formatting | bytes 104857600
  149.2 3.2 fusion.51
  152.4 39.9 %all-reduce = (f32[2,1024]{1,0:T(2,128)S(1)}, f32[2,1024]{1,0:T(2,128)S(1)}) all-reduce(f32[2,1024]{1,0:T(2,128)S(1)} %get-tuple-element.6, f32[2,1024]{1,0:T(2,128)S(1)} %get-tuple-element.5), channel_id=1, replica_groups=mesh['ckpt'=2,'fsdp'=8,'dp'=2] {'fsdp'}, use_global_device_ids=true, to_apply=%region_3.0 | all-reduce | flops 4096 | bytes 32768 | tf_op jit(solution)/shard_map/psum | solution.py:34
  192.3 5.1 fusion.54
  197.4 0.1 compare_and_fusion
  197.5 8.1 fusion.62
  205.6 5.3 stack.10
  210.9 8.2 fusion.59
  219.1 6.6 stack.9
  225.6 2.5 fusion.96
  228.2 34.5 %fusion.65 = bf16[2,800,2048]{2,1,0:T(8,128)(2,1)} fusion(f32[2048]{0:T(1024)S(1)} %subtract_convert_fusion, bf16[2,800,2048]{2,1,0:T(8,128)(2,1)S(1)} %fusion.96), kind=kOutput, calls=%fused_computation.82 | convolution fusion | flops 13597016064 | bytes 13115392 | tf_op jit(solution)/shard_map/lws,sv->lwv/dot_general | solution.py:57
  262.7 18.7 %copy.8 = bf16[2,800,2048]{1,0,2:T(2,128)(2,1)} copy(bf16[2,800,2048]{2,1,0:T(8,128)(2,1)} %fusion.65) | data formatting | bytes 13107200 | tf_op jit(solution)/shard_map/convert_element_type | solution.py:59
  281.4 227.9 %gather_fusion = bf16[16384,2,800]{2,1,0:T(2,128)(2,1)} fusion(bf16[2,800,2048]{1,0,2:T(2,128)(2,1)} %copy.8, s32[16384]{0:T(1024)S(1)} %get-tuple-element.11), kind=kCustom, calls=%fused_computation | custom fusion | bytes 104923136 | tf_op jit(solution)/shard_map/jit(_take)/gather | solution.py:67
  509.3 239.9 %multiply_reduce_fusion = f32[16384,2]{1,0:T(8,128)} fusion(f32[16384,800]{1,0:T(8,128)} %copy.17, bf16[16384,2,800]{2,1,0:T(2,128)(2,1)} %gather_fusion, pred[16384]{0:T(1024)(128)(4,1)S(1)} %compare_and_fusion), kind=kLoop, calls=%fused_computation.15 | loop fusion | flops 104824832 | bytes 105005056
  749.2 5.8 broadcast_multiply_fusion
  755.0 5.3 copy.18
  760.3 4.9 copy.15
  765.3 146.3 %reduce-scatter.4.cloned.1.call-done = f32[2048,2]{1,0:T(8,128)} async-done(((f32[16384,2]{1,0:T(8,128)}), f32[2048,2]{1,0:T(8,128)}) %reduce-scatter.4.cloned.1.call-update) | async-done | bytes 16400
  911.6 2.2 copy.16
  (18 shorter events, 0.2 us)
Async XLA Ops:
  6.5 190.9 %all-gather.7.cloned.1.call-start = ((), (), s32[]{:S(2)}) async-start(), calls=%async_computation.2 | async-start | bytes 5898240 | tf_op jit(solution)/shard_map/all_gather | solution.py:47
  9.0 201.9 %all-gather.5.cloned.1.call-start = ((), (), s32[]{:S(2)}) async-start(), calls=%async_computation.1 | async-start | bytes 5898240 | tf_op jit(solution)/shard_map/all_gather | solution.py:47
  9.8 901.8 %reduce-scatter.4.cloned.1.call-start = ((), (), s32[]{:S(2)}) async-start(), calls=%async_computation.3 | async-start | bytes 9437184
  90.7 58.5 %copy-start.3 = (bf16[640]{0:T(1024)(128)(2,1)S(1)}, bf16[640]{0:T(1024)(128)(2,1)}, u32[]{:S(2)}) copy-start(bf16[640]{0:T(1024)(128)(2,1)} %param.10) | copy-start | bytes 3844
  90.7 58.5 %copy-start = (bf16[2,640,1024]{2,1,0:T(8,128)(2,1)S(1)}, bf16[2,640,1024]{2,1,0:T(8,128)(2,1)}, u32[]{:S(2)}) copy-start(bf16[2,640,1024]{2,1,0:T(8,128)(2,1)} %param.7) | copy-start | bytes 7864324
  90.7 101.6 %copy-start.2 = (s32[2048]{0:T(1024)S(1)}, s32[2048]{0:T(1024)}, u32[]{:S(2)}) copy-start(s32[2048]{0:T(1024)} %param.12) | copy-start | bytes 24580
  90.7 106.7 %copy-start.1 = (s32[16384]{0:T(1024)S(1)}, s32[16384]{0:T(1024)}, u32[]{:S(2)}) copy-start(s32[16384]{0:T(1024)} %param.13) | copy-start | bytes 196612
Sparse Core Ops, SparseCore 0:
  9.5 88.9 all-gather.6
  100.7 85.1 all-gather.4
  765.4 146.1 reduce-scatter.3
where the time goes:
time: 933 us; the launch traced here: 921 us
  other arithmetic  337 us (36%)
  local copies, waits for them, and re-layouts  332 us (36%)
  waiting for transfers between devices  147 us (16%)
  matrix products  50.8 us (5%)
  blocking collectives  39.9 us (4%)
  between operations  13.6 us (1%)
    unnamed x2, other arithmetic  319 us
    gather x1, local copies, waits for them, and re-layouts, on_device(): picked = jnp.take(mixed_rows, kept_col, axis=2).astype(jnp.float32)  228 us
    unnamed x4, waiting for transfers between devices  147 us
    unnamed x12, local copies, waits for them, and re-layouts  70.9 us
    psum x1, blocking collectives, on_device(): lax.psum((jnp.sum(hidden * hidden, axis=1), jnp.sum(weighted * hidden, ax...  39.9 us
    dot_general x1, matrix products, on_device(): jnp.einsum('lws,sv->lwv', zero_padded_rows, sign_lookup_matrix, preferred...  34.5 us
    convert_element_type x1, local copies, waits for them, and re-layouts, on_device(): mixed_rows = jnp.einsum('lws,sv->lwv', zero_padded_rows, sign_lookup_matr...  18.7 us
  transfers between devices with their start and end apart: 3, of which 1 were waited for; matrix products, arithmetic and copies ran while one was open for 17% of the time, Pallas kernels for 0%

commit v1 on v0

v1 whole, which is shorter than its diff:
```python
import functools
import math

import jax
import jax.numpy as jnp
import numpy as np
from jax import lax
from jax.experimental import pallas as pl
from jax.experimental.pallas import tpu as pltpu
from jax.sharding import PartitionSpec as P

EPS = 1e-06
GROUPS = 50
HALF = 64
SEG = 512
LOW = 256
NT = (((1,), (1,)), ((), ()))


def hadamard_np(order):
    h = np.ones((1, 1), np.float32)
    while h.shape[0] < order:
        h = np.block([[h, h], [h, -h]])
    return h


def parity(values):
    for shift in (8, 4, 2, 1):
        values = values ^ (values >> shift)
    return values & 1


def dot_nt(a, b):
    return lax.dot_general(a, b, NT, preferred_element_type=jnp.float32)


def project_kernel(
    low_rows, cols, span, row_pad, pos_ref, kept_ref, kept_rows_ref, g_ref, c_ref, b_ref, l_ref, h_ref, eye_ref,
    out_ref, x_ref, table_ref, buf_ref,
):
    segs = c_ref.shape[1] // SEG
    parts = cols // SEG
    for e in range(2):
        for nb in range(segs):
            block = dot_nt(g_ref[e], c_ref[e, nb * SEG : (nb + 1) * SEG, :])
            for gamma in range(parts):
                omega, sigma = divmod(segs * gamma + nb, parts)
                signed = block[gamma * row_pad : (gamma + 1) * row_pad] * b_ref[0:1, sigma * SEG : (sigma + 1) * SEG]
                x_ref[e, omega * row_pad : (omega + 1) * row_pad, sigma * SEG : (sigma + 1) * SEG] = signed.astype(
                    jnp.bfloat16
                )
    per_step = min(low_rows, 4)
    high = cols // LOW

    def table_step(step, carry):
        start = pl.multiple_of(step * (per_step * HALF), per_step * HALF)
        mixed = []
        for e in range(2):
            t = jnp.dot(l_ref[pl.ds(start, per_step * HALF), :], x_ref[e], preferred_element_type=jnp.float32)
            blocks = [t[:, h * LOW : (h + 1) * LOW] for h in range(high)]
            width = 1
            while width < high:
                new = list(blocks)
                for h in range(high):
                    if h & width == 0:
                        new[h] = blocks[h] + blocks[h | width]
                        new[h | width] = blocks[h] - blocks[h | width]
                blocks = new
                width *= 2
            mixed.append([v.astype(jnp.bfloat16) for v in blocks])
        for h in range(high):
            y = jnp.concatenate(
                [mixed[e][h][p * HALF : (p + 1) * HALF] for p in range(per_step) for e in range(2)], axis=0
            )
            r = dot_nt(h_ref[...], y)
            for p in range(per_step):
                row = pl.multiple_of((step * per_step + p) * cols + h * LOW, LOW)
                table_ref[pl.ds(row, LOW), :] = r[:, p * 2 * HALF : (p + 1) * 2 * HALF]
        return carry

    lax.fori_loop(0, low_rows // per_step, table_step, 0)

    shift = (low_rows * cols).bit_length() - 1
    mask = low_rows * cols - 1
    first_group = pos_ref[0] * GROUPS
    unroll = 32

    def pick_step(chunk, carry):
        def rows(group, inner):
            base = pl.multiple_of(group * unroll, unroll)
            for u in range(unroll):
                index = kept_ref[chunk * span + base + u] & mask
                buf_ref[pl.ds(base + u, 1), :] = table_ref[pl.ds(index, 1), :]
            return inner

        lax.fori_loop(0, span // unroll, rows, 0)
        values = buf_ref[...]
        upper = values.astype(jnp.bfloat16)
        lower = (values - upper.astype(jnp.float32)).astype(jnp.bfloat16)
        turned = dot_nt(eye_ref[...], upper) + dot_nt(eye_ref[...], lower)
        kept_high = kept_rows_ref[pl.ds(chunk, 1), :] >> shift
        group_index = lax.broadcasted_iota(jnp.int32, (HALF, span), 0) + first_group
        sign = (1 - 2 * parity(group_index & kept_high)).astype(jnp.float32)
        for e in range(2):
            total = jnp.sum(turned[e * HALF : (e + 1) * HALF] * sign, axis=0, keepdims=True)
            out_ref[chunk, e : e + 1, :] = total
        return carry

    lax.fori_loop(0, kept_rows_ref.shape[0], pick_step, 0)


def scatter_kernel(n, scale, in_ref, out_ref, land_ref, send_sem, recv_sem):
    me = lax.axis_index("fsdp")
    barrier = pltpu.get_barrier_semaphore()
    for k in range(1, n):
        pl.semaphore_signal(
            barrier, inc=1, device_id={"fsdp": lax.rem(me + k, n)}, device_id_type=pl.DeviceIdType.MESH
        )
    pl.semaphore_wait(barrier, n - 1)
    copies = []
    for k in range(1, n):
        peer = lax.rem(me + k, n)
        copy = pltpu.make_async_remote_copy(
            src_ref=in_ref.at[peer],
            dst_ref=land_ref.at[k - 1],
            send_sem=send_sem.at[k - 1],
            recv_sem=recv_sem.at[k - 1],
            device_id={"fsdp": peer},
            device_id_type=pl.DeviceIdType.MESH,
        )
        copy.start()
        copies.append(copy)
    total = in_ref[me]
    for k, copy in enumerate(copies):
        copy.wait()
        total = total + land_ref[k]
    out_ref[...] = total * scale


def on_device(n, hidden_in, cotangent, context, norm_gain, signs_rows, column_sign_flips, kept_index):
    pos = lax.axis_index("fsdp")
    examples, local_d, seq = hidden_in.shape
    d_total = local_d * n
    rows_a, cols, kept = signs_rows.shape[0], column_sign_flips.shape[0], kept_index.shape[0]
    hc = context.shape[1] * n
    local_rows = local_d * hc // cols
    low_rows = local_rows // GROUPS
    parts, segs = cols // SEG, hc // SEG
    deltas = local_d // parts
    row_pad = -(-deltas // 16) * 16

    hidden = hidden_in.astype(jnp.float32)
    weighted = norm_gain.astype(jnp.float32)[None, :, None] * cotangent.astype(jnp.float32)
    square_sum, cross_sum = lax.psum(
        (jnp.sum(hidden * hidden, axis=1), jnp.sum(weighted * hidden, axis=1)), "fsdp"
    )
    inverse = lax.rsqrt(square_sum / d_total + EPS)
    grad_hidden = (
        weighted * inverse[:, None, :] - hidden * (cross_sum * inverse**3 / d_total)[:, None, :]
    ).astype(jnp.bfloat16)
    g = grad_hidden.reshape(examples, deltas, parts, seq).transpose(0, 2, 1, 3)
    g = jnp.pad(g, ((0, 0), (0, 0), (0, row_pad - deltas), (0, 0))).reshape(examples, parts * row_pad, seq)
    full_context = lax.all_gather(context, "fsdp", axis=1, tiled=True)

    sign_b = (1 - 2 * column_sign_flips).astype(jnp.float32)[None, :]
    delta = np.arange(row_pad)
    w = segs * delta[None, :] + np.arange(segs)[:, None]
    live = np.broadcast_to(delta[None, :] < deltas, w.shape).reshape(-1)
    w = np.where(live, w.reshape(-1), 0)
    local_flips = lax.dynamic_slice_in_dim(signs_rows, pos * local_rows, local_rows, 0)
    flips = local_flips.reshape(deltas, segs).T
    flips = jnp.pad(flips, ((0, 0), (0, row_pad - deltas))).reshape(-1)
    sign_a = (1 - 2 * flips).astype(jnp.bfloat16)
    ham = hadamard_np(low_rows)[:, w % low_rows]
    member = (np.arange(HALF)[:, None] == (w // low_rows)[None, :]) & live[None, :]
    l = (ham[:, None, :] * member[None, :, :]).reshape(low_rows * HALF, segs * row_pad)
    l = jnp.asarray(l.astype(np.int8)).astype(jnp.bfloat16) * sign_a[None, :]

    span = min(512, kept // n)
    chunks = kept // span
    vmem = pl.BlockSpec(memory_space=pltpu.VMEM)
    smem = pl.BlockSpec(memory_space=pltpu.SMEM)
    partial = pl.pallas_call(
        functools.partial(project_kernel, low_rows, cols, span, row_pad),
        out_shape=jax.ShapeDtypeStruct((chunks, 2, span), jnp.float32),
        in_specs=[smem, smem] + [vmem] * 7,
        out_specs=vmem,
        scratch_shapes=[
            pltpu.VMEM((2, segs * row_pad, cols), jnp.bfloat16),
            pltpu.VMEM((low_rows * cols, 2 * HALF), jnp.float32),
            pltpu.VMEM((span, 2 * HALF), jnp.float32),
        ],
        compiler_params=pltpu.CompilerParams(vmem_limit_bytes=58 * 2**20),
        name="project",
    )(
        pos.reshape(1),
        kept_index,
        kept_index.reshape(chunks, span),
        g,
        full_context,
        sign_b,
        l,
        jnp.asarray(hadamard_np(LOW), jnp.bfloat16),
        jnp.eye(2 * HALF, dtype=jnp.bfloat16),
    )
    own = chunks // n
    scale = 1.0 / math.sqrt(rows_a * cols * seq)
    total = pl.pallas_call(
        functools.partial(scatter_kernel, n, scale),
        out_shape=jax.ShapeDtypeStruct((own * 2, span), jnp.float32),
        in_specs=[vmem],
        out_specs=vmem,
        scratch_shapes=[
            pltpu.VMEM((n - 1, own * 2, span), jnp.float32),
            pltpu.SemaphoreType.DMA((n - 1,)),
            pltpu.SemaphoreType.DMA((n - 1,)),
        ],
        compiler_params=pltpu.CompilerParams(collective_id=0, has_side_effects=True),
        name="scatter_sum",
    )(partial.reshape(n, own * 2, span))
    return total.reshape(own, 2, span).transpose(1, 0, 2).reshape(2, own * span)


def solution(mesh):
    return jax.shard_map(
        functools.partial(on_device, mesh.shape["fsdp"]),
        mesh=mesh,
        in_specs=(
            P(("ckpt", "dp"), "fsdp", None),
            P(("ckpt", "dp"), "fsdp", None),
            P(("ckpt", "dp"), "fsdp", None),
            P("fsdp"),
            P(),
            P(),
            P(),
        ),
        out_specs=P(("ckpt", "dp"), "fsdp"),
        check_vma=False,
    )
```

time: 933 us -> 235 us (0.25); the launches traced: 921 us -> 234 us
  other arithmetic: 337 us -> 12.5 us
  local copies, waits for them, and re-layouts: 332 us -> 11.3 us
  Pallas kernels: 0 us -> 61.1 us
  matrix products: 50.8 us -> 0 us
  waiting for transfers between devices: 147 us -> 96.2 us
    unnamed x2 -> x0, other arithmetic: 319 us -> none
    gather x1 -> x0, local copies, waits for them, and re-layouts: 228 us -> none  [on_device(): picked = jnp.take(mixed_rows, kept_col, axis=2).astype(jnp.float32)]
    unnamed x4 -> x1, waiting for transfers between devices: 147 us -> 0.71 us
    all_gather x2 -> x1, waiting for transfers between devices: 0.04 us -> 95.5 us  [on_device(): full_context = lax.all_gather(context, 'fsdp', axis=1, tiled=True)]
    unnamed x12 -> x6, local copies, waits for them, and re-layouts: 70.9 us -> 0.02 us
    pallas_call x0 -> x2, Pallas kernels: none -> 61.1 us  [the longest x1 53 us: on_device(): pl.pallas_call(functools.partial(project_kernel, low_rows, cols, span, ro...]
    dot_general x3 -> x0, matrix products: 50.8 us -> none  [the longest x1 34.5 us: on_device(): jnp.einsum('lws,sv->lwv', zero_padded_rows, sign_lookup_matrix, preferred...]
    convert_element_type x1 -> x2, local copies, waits for them, and re-layouts: 18.7 us -> 0.18 us  [on_device(): sign_a = (1 - 2 * flips).astype(jnp.bfloat16)]
  transfers between devices with their start and end apart: 3 -> 1, of which waited for: 1 -> 1; matrix products, arithmetic and copies ran while one was open for 17% -> 9% of each run, Pallas kernels for 0% -> 0%
where the time goes in v1:
time: 235 us; the launch traced here: 234 us
  waiting for transfers between devices  96.2 us (41%)
  Pallas kernels  61.1 us (26%)
  blocking collectives  39.9 us (17%)
  between operations  13.4 us (6%)
  other arithmetic  12.5 us (5%)
  local copies, waits for them, and re-layouts  11.3 us (5%)
    all_gather x1, waiting for transfers between devices, on_device(): full_context = lax.all_gather(context, 'fsdp', axis=1, tiled=True)  95.5 us
    pallas_call x1, Pallas kernels, on_device(): pl.pallas_call(functools.partial(project_kernel, low_rows, cols, span, ro...  53 us
    psum x1, blocking collectives, on_device(): lax.psum((jnp.sum(hidden * hidden, axis=1), jnp.sum(weighted * hidden, ax...  39.9 us
    pallas_call x1, Pallas kernels, on_device(): pl.pallas_call(functools.partial(scatter_kernel, n, scale), out_shape=jax...  8.09 us
    reshape x2, local copies, waits for them, and re-layouts, on_device(): g = grad_hidden.reshape(examples, deltas, parts, seq).transpose(0, 2, 1, 3)  7.27 us
  transfers between devices with their start and end apart: 1, of which 1 were waited for; matrix products, arithmetic and copies ran while one was open for 9% of the time, Pallas kernels for 0%

profile of v1, /device:TPU:0, one launch (start us, length us, event | category | flops | bytes accessed | tf_op | source)
XLA Modules:
  0.0 234.5 jit_solution(753314757686310980)
XLA Ops:
  6.5 0.0 all-gather.2.cloned.1.call-start
  6.5 0.7 all-gather.2.cloned.1.call-update
  7.3 0.7 convert_element_type.32
  7.9 4.0 %fusion = (f32[2,1024]{1,0:T(2,128)S(1)}, f32[2,1024]{1,0:T(2,128)S(1)}) fusion(bf16[2,640,1024]{2,1,0:T(8,128)(2,1)} %param.9, bf16[2,640,1024]{2,1,0:T(8,128)(2,1)} %param.10, f32[640]{0:T(1024)S(1)} %convert_element_type.32), kind=kLoop, calls=%fused_computation.3 | loop fusion | flops 9170944 | bytes 5261824 | tf_op jit(solution)/shard_map/reduce_sum | solution.py:155
  11.9 39.9 %all-reduce = (f32[2,1024]{1,0:T(2,128)S(1)}, f32[2,1024]{1,0:T(2,128)S(1)}) all-reduce(f32[2,1024]{1,0:T(2,128)S(1)} %get-tuple-element.6, f32[2,1024]{1,0:T(2,128)S(1)} %get-tuple-element.5), channel_id=1, replica_groups=mesh['ckpt'=2,'fsdp'=8,'dp'=2] {'fsdp'}, use_global_device_ids=true, to_apply=%region_3.0 | all-reduce | flops 4096 | bytes 32768 | tf_op jit(solution)/shard_map/psum | solution.py:154
  51.8 4.4 %fusion.3 = bf16[2,640,1024]{2,1,0:T(8,128)(2,1)S(1)} fusion(bf16[2,640,1024]{2,1,0:T(8,128)(2,1)} %param.9, bf16[2,640,1024]{2,1,0:T(8,128)(2,1)} %param.10, f32[2,1024]{1,0:T(2,128)S(1)} %get-tuple-element.10, f32[2,1024]{1,0:T(2,128)S(1)} %get-tuple-element.9, f32[640]{0:T(1024)S(1)} %convert_element_type.32), kind=kLoop, calls=%fused_computation.6 | loop fusion | flops 9175040 | bytes 7883264 | tf_op jit(solution)/shard_map/convert_element_type | solution.py:160
  56.2 0.0 copy-start.1
  56.3 0.0 copy-start.2
  56.3 3.1 %reshape.45 = bf16[2,160,4,1024]{3,2,1,0:T(4,128)(2,1)} reshape(bf16[2,640,1024]{2,1,0:T(8,128)(2,1)S(1)} %fusion.3) | data formatting | bytes 5242880 | tf_op jit(solution)/shard_map/reshape | solution.py:161
  59.3 4.2 %copy.12 = bf16[2,160,4,1024]{3,1,2,0:T(8,128)(2,1)} copy(bf16[2,160,4,1024]{3,2,1,0:T(4,128)(2,1)} %reshape.45) | data formatting | bytes 5242880 | tf_op jit(solution)/shard_map/reshape | solution.py:161
  63.5 0.8 subtract_convert_fusion.1
  64.3 0.2 sub.29
  64.5 0.1 copy.13
  64.6 0.1 convert_element_type.39
  64.7 0.0 copy-done.1
  64.7 0.6 reshape.44.kept_rows_ref
  65.4 0.6 fusion.4.eye_ref
  66.0 0.6 subtract_convert_fusion
  66.6 1.4 broadcast_multiply_fusion.l_ref
  68.0 95.5 %all-gather.2.cloned.1.call-done.c_ref = bf16[2,2560,1024]{2,1,0:T(8,128)(2,1)} async-done(((bf16[2,320,1024]{2,1,0:T(8,128)(2,1)}), bf16[2,2560,1024]{2,1,0:T(8,128)(2,1)}) %all-gather.2.cloned.1.call-update) | async-done | bytes 10485776 | tf_op jit(solution)/shard_map/all_gather | solution.py:163
  163.5 53.0 %project.1 = f32[32,2,512]{2,1,0:T(2,128)} custom-call(s32[1]{0:T(128)} %bitcast.pos_ref, s32[16384]{0:T(1024)} %kept_ref.1, s32[32,512]{1,0:T(8,128)} %reshape.44.kept_rows_ref, bf16[2,640,1024]{2,1,0:T(8,128)(2,1)} %bitcast.9, bf16[2,2560,1024]{2,1,0:T(8,128)(2,1)} %all-gather.2.cloned.1.call-done.c_ref, f32[1,2048]{1,0:T(1,128)} %bitcast.11, ...), custom_call_target="tpu_custom_call" | custom-call | tf_op jit(solution)/shard_map/project/pallas_call | solution.py:183
  216.6 1.6 reshape.47.in_ref
  218.2 8.1 %scatter_sum.1 = f32[8,512]{1,0:T(8,128)} custom-call(f32[8,8,512]{2,1,0:T(8,128)} %reshape.47.in_ref), custom_call_target="tpu_custom_call" | custom-call | tf_op jit(solution)/shard_map/scatter_sum/pallas_call | solution.py:208
  226.3 1.3 reshape.48
  (4 shorter events, 0.0 us)
Async XLA Ops:
  6.5 157.0 %all-gather.2.cloned.1.call-start = ((), (), s32[]{:S(2)}) async-start(), calls=%async_computation | async-start | bytes 11796480 | tf_op jit(solution)/shard_map/all_gather | solution.py:163
  56.2 8.5 %copy-start.1 = (s32[16384]{0:T(1024)S(1)}, s32[16384]{0:T(1024)}, u32[]{:S(2)}) copy-start(s32[16384]{0:T(1024)} %kept_ref.1) | copy-start | bytes 196612
  56.3 9.7 %copy-start.2 = (s32[2048]{0:T(1024)S(1)}, s32[2048]{0:T(1024)}, u32[]{:S(2)}) copy-start(s32[2048]{0:T(1024)} %param.14) | copy-start | bytes 24580
  59.3 7.3 %copy-start = (bf16[1024,800]{1,0:T(8,128)(2,1)S(1)}, bf16[1024,800]{1,0:T(8,128)(2,1)}, u32[]{:S(2)}) copy-start(bf16[1024,800]{1,0:T(8,128)(2,1)} %constant.35) | copy-start | bytes 4915204
Sparse Core Ops, SparseCore 0:
  9.5 153.9 all-gather.1

commit v2 on v1

v2 whole, which is shorter than its diff:
```python
import functools
import math

import jax
import jax.numpy as jnp
import numpy as np
from jax import lax
from jax.experimental import pallas as pl
from jax.experimental.pallas import tpu as pltpu
from jax.sharding import PartitionSpec as P

EPS = 1e-06
GROUPS = 50
HALF = 64
SEG = 512
LOW = 256
NT = (((1,), (1,)), ((), ()))


def hadamard_np(order):
    h = np.ones((1, 1), np.float32)
    while h.shape[0] < order:
        h = np.block([[h, h], [h, -h]])
    return h


def parity(values):
    for shift in (8, 4, 2, 1):
        values = values ^ (values >> shift)
    return values & 1


def dot_nt(a, b):
    return lax.dot_general(a, b, NT, preferred_element_type=jnp.float32)


def project_kernel(
    low_rows, cols, span, row_pad, pos_ref, kept_ref, kept_rows_ref, g_ref, c_ref, b_ref, l_ref, h_ref, eye_ref,
    out_ref, x_ref, table_ref, buf_ref,
):
    segs = c_ref.shape[0] // SEG
    parts = cols // SEG
    for e in range(2):
        for nb in range(segs):
            block = dot_nt(g_ref[e], c_ref[nb * SEG : (nb + 1) * SEG, :])
            for gamma in range(parts):
                omega, sigma = divmod(segs * gamma + nb, parts)
                signed = block[gamma * row_pad : (gamma + 1) * row_pad] * b_ref[0:1, sigma * SEG : (sigma + 1) * SEG]
                x_ref[e, omega * row_pad : (omega + 1) * row_pad, sigma * SEG : (sigma + 1) * SEG] = signed.astype(
                    jnp.bfloat16
                )
    per_step = min(low_rows, 4)
    high = cols // LOW

    def table_step(step, carry):
        start = pl.multiple_of(step * (per_step * HALF), per_step * HALF)
        mixed = []
        for e in range(2):
            t = jnp.dot(l_ref[e, pl.ds(start, per_step * HALF), :], x_ref[e], preferred_element_type=jnp.float32)
            blocks = [t[:, h * LOW : (h + 1) * LOW] for h in range(high)]
            width = 1
            while width < high:
                new = list(blocks)
                for h in range(high):
                    if h & width == 0:
                        new[h] = blocks[h] + blocks[h | width]
                        new[h | width] = blocks[h] - blocks[h | width]
                blocks = new
                width *= 2
            mixed.append([v.astype(jnp.bfloat16) for v in blocks])
        for h in range(high):
            y = jnp.concatenate(
                [mixed[e][h][p * HALF : (p + 1) * HALF] for p in range(per_step) for e in range(2)], axis=0
            )
            r = dot_nt(h_ref[...], y)
            for p in range(per_step):
                row = pl.multiple_of((step * per_step + p) * cols + h * LOW, LOW)
                table_ref[pl.ds(row, LOW), :] = r[:, p * 2 * HALF : (p + 1) * 2 * HALF]
        return carry

    lax.fori_loop(0, low_rows // per_step, table_step, 0)

    shift = (low_rows * cols).bit_length() - 1
    mask = low_rows * cols - 1
    first_group = pos_ref[0] * GROUPS
    unroll = 32

    def pick_step(chunk, carry):
        def rows(group, inner):
            base = pl.multiple_of(group * unroll, unroll)
            for u in range(unroll):
                index = kept_ref[chunk * span + base + u] & mask
                buf_ref[pl.ds(base + u, 1), :] = table_ref[pl.ds(index, 1), :]
            return inner

        lax.fori_loop(0, span // unroll, rows, 0)
        values = buf_ref[...]
        upper = values.astype(jnp.bfloat16)
        lower = (values - upper.astype(jnp.float32)).astype(jnp.bfloat16)
        turned = dot_nt(eye_ref[...], upper) + dot_nt(eye_ref[...], lower)
        kept_high = kept_rows_ref[pl.ds(chunk, 1), :] >> shift
        lane = lax.broadcasted_iota(jnp.int32, (2 * HALF, span), 0)
        group_index = first_group + jnp.where(lane >= HALF, lane + (GROUPS - HALF), lane)
        sign = (1 - 2 * parity(group_index & kept_high)).astype(jnp.float32)
        own = out_ref.shape[1]
        out_ref[chunk // own, pl.ds(lax.rem(chunk, own), 1), :] = jnp.sum(turned * sign, axis=0, keepdims=True)
        return carry

    lax.fori_loop(0, kept_rows_ref.shape[0], pick_step, 0)


def greet(n, me):
    barrier = pltpu.get_barrier_semaphore()
    for k in range(1, n):
        pl.semaphore_signal(
            barrier, inc=1, device_id={"fsdp": lax.rem(me + k, n)}, device_id_type=pl.DeviceIdType.MESH
        )
    pl.semaphore_wait(barrier, n - 1)


def remote(src, dst, send_sem, recv_sem, peer):
    return pltpu.make_async_remote_copy(
        src_ref=src,
        dst_ref=dst,
        send_sem=send_sem,
        recv_sem=recv_sem,
        device_id={"fsdp": peer},
        device_id_type=pl.DeviceIdType.MESH,
    )


def exchange_kernel(
    n, d_total, row_pad, hidden_ref, cot_ref, gain_ref, context_ref, c_ref, g_ref,
    stats_ref, whole_ref, land_ref, stage_ref, gbuf_ref,
    stat_send, stat_recv, pair_send, pair_recv, right_send, right_recv, left_send, left_recv, local_sem,
):
    me = lax.axis_index("fsdp")
    y = lax.rem(me, 2)
    z = me // 2
    nz = n // 2
    partner = me + 1 - 2 * y
    local_d, seq = hidden_ref.shape[1:]
    parts = gbuf_ref.shape[1] // row_pad
    greet(n, me)

    def right(step, sub):
        half = y if sub == 0 else 1 - y
        block = lax.max(z - step, 0)
        src = context_ref.at[y] if step == 0 and sub == 0 else c_ref.at[block, half]
        return remote(
            src, c_ref.at[block, half], right_send.at[step, sub], right_recv.at[step, sub], lax.min(me + 2, n - 1)
        )

    def left(step, sub):
        half = y if sub == 0 else 1 - y
        block = lax.min(z + step, nz - 1)
        src = context_ref.at[y] if step == 0 and sub == 0 else c_ref.at[block, half]
        return remote(
            src, c_ref.at[block, half], left_send.at[step, sub], left_recv.at[step, sub], lax.max(me - 2, 0)
        )

    def sends_right(step):
        return jnp.logical_and(z < nz - 1, z >= step)

    def sends_left(step):
        return jnp.logical_and(z > 0, z + step < nz)

    def start_both(step, sub):
        @pl.when(sends_right(step))
        def _():
            right(step, sub).start()

        @pl.when(sends_left(step))
        def _():
            left(step, sub).start()

    swap = remote(context_ref.at[1 - y], c_ref.at[z, y], pair_send.at[0], pair_recv.at[0], partner)
    swap.start()
    start_both(0, 0)
    keep = pltpu.make_async_copy(context_ref.at[y], c_ref.at[z, y], local_sem.at[0])
    keep.start()

    rows = 32

    def add_rows(tile, carry):
        start = pl.multiple_of(tile * rows, rows)
        gain = gain_ref[pl.ds(start, rows), :]
        out = []
        for e in range(2):
            h = hidden_ref[e, pl.ds(start, rows), :].astype(jnp.float32)
            w = cot_ref[e, pl.ds(start, rows), :].astype(jnp.float32) * gain
            out.append(carry[2 * e] + jnp.sum((h * h).reshape(rows // 8, 8, seq), axis=0))
            out.append(carry[2 * e + 1] + jnp.sum((w * h).reshape(rows // 8, 8, seq), axis=0))
        return tuple(out)

    sums = lax.fori_loop(0, local_d // rows, add_rows, (jnp.zeros((8, seq), jnp.float32),) * 4)
    for k in range(4):
        stats_ref[k : k + 1, :] = jnp.sum(sums[k], axis=0, keepdims=True)
    stats_ref[4:8, :] = jnp.zeros((4, seq), jnp.float32)
    stat_copies = []
    for k in range(1, n):
        copy = remote(
            stats_ref, land_ref.at[k], stat_send.at[k], stat_recv.at[k], lax.rem(me + k, n)
        )
        copy.start()
        stat_copies.append(copy)
    swap.wait_recv()
    start_both(0, 1)
    land_ref[0] = stats_ref[...]
    for copy in stat_copies:
        copy.wait_recv()
    total = land_ref[0]
    for k in range(1, n):
        total = total + land_ref[k]
    for copy in stat_copies:
        copy.wait_send()
    for k in range(4):
        whole_ref[k] = total[k : k + 1, :]

    stage_ref[...] = jnp.zeros_like(stage_ref)

    def gradient_of(e, slot):
        def tokens(tile, carry):
            lanes = pl.ds(pl.multiple_of(tile * 128, 128), 128)
            inverse = lax.rsqrt(whole_ref[2 * e, :, lanes] / d_total + EPS)
            factor = whole_ref[2 * e + 1, :, lanes] * inverse * inverse * inverse / d_total
            h = hidden_ref[e, :, lanes].astype(jnp.float32)
            w = cot_ref[e, :, lanes].astype(jnp.float32) * gain_ref[...]
            stage_ref[0:local_d, :] = w * inverse - h * factor
            for gamma in range(parts):
                picked = stage_ref[pl.ds(gamma, row_pad, stride=parts), :]
                gbuf_ref[slot, gamma * row_pad : (gamma + 1) * row_pad, lanes] = picked.astype(jnp.bfloat16)
            return carry

        lax.fori_loop(0, seq // 128, tokens, 0)

    gradient_of(1 - y, 0)
    give = remote(gbuf_ref.at[0], g_ref.at[y], pair_send.at[1], pair_recv.at[1], partner)
    give.start()
    gradient_of(y, 1)
    hold = pltpu.make_async_copy(gbuf_ref.at[1], g_ref.at[y], local_sem.at[1])
    hold.start()

    for step in range(nz - 1):
        for sub in range(2):
            @pl.when(z >= step + 1)
            def _():
                right(step, sub).wait_recv()

            @pl.when(z + step + 1 < nz)
            def _():
                left(step, sub).wait_recv()

            if step + 1 < nz - 1:
                start_both(step + 1, sub)
    for step in range(nz - 1):
        for sub in range(2):

            @pl.when(sends_right(step))
            def _():
                right(step, sub).wait_send()

            @pl.when(sends_left(step))
            def _():
                left(step, sub).wait_send()

    swap.wait_send()
    keep.wait()
    give.wait()
    hold.wait()


def scatter_kernel(n, scale, in_ref, out_ref, land_ref, send_sem, recv_sem):
    me = lax.axis_index("fsdp")
    y = lax.rem(me, 2)
    greet(n, me)
    copies = []
    for k in range(1, n):
        peer = lax.rem(me + k, n)
        copy = remote(in_ref.at[peer], land_ref.at[k - 1], send_sem.at[k - 1], recv_sem.at[k - 1], peer)
        copy.start()
        copies.append(copy)
    totals = [in_ref[me], None]
    for k in range(1, n):
        copies[k - 1].wait()
        value = land_ref[k - 1]
        totals[k % 2] = value if totals[k % 2] is None else totals[k % 2] + value
    out_ref[y] = totals[0] * scale
    out_ref[1 - y] = totals[1] * scale


def on_device(n, hidden_in, cotangent, context, norm_gain, signs_rows, column_sign_flips, kept_index):
    pos = lax.axis_index("fsdp")
    local_d, seq = hidden_in.shape[1:]
    d_total = local_d * n
    rows_a, cols, kept = signs_rows.shape[0], column_sign_flips.shape[0], kept_index.shape[0]
    local_hc = context.shape[1]
    hc = local_hc * n
    local_rows = local_d * hc // cols
    low_rows = local_rows // GROUPS
    parts, segs = cols // SEG, hc // SEG
    deltas = local_d // parts
    row_pad = -(-deltas // 16) * 16
    vmem = pl.BlockSpec(memory_space=pltpu.VMEM)
    smem = pl.BlockSpec(memory_space=pltpu.SMEM)
    anywhere = pl.BlockSpec(memory_space=pl.ANY)
    dma = pltpu.SemaphoreType.DMA
    nz = n // 2

    full_context, g = pl.pallas_call(
        functools.partial(exchange_kernel, n, d_total, row_pad),
        out_shape=(
            jax.ShapeDtypeStruct((nz, 2, local_hc, seq), jnp.bfloat16),
            jax.ShapeDtypeStruct((2, parts * row_pad, seq), jnp.bfloat16),
        ),
        in_specs=[vmem, vmem, vmem, anywhere],
        out_specs=(anywhere, anywhere),
        scratch_shapes=[
            pltpu.VMEM((8, seq), jnp.float32),
            pltpu.VMEM((4, 1, seq), jnp.float32),
            pltpu.VMEM((n, 8, seq), jnp.float32),
            pltpu.VMEM((parts * row_pad, 128), jnp.float32),
            pltpu.VMEM((2, parts * row_pad, seq), jnp.bfloat16),
            dma((n,)),
            dma((n,)),
            dma((2,)),
            dma((2,)),
            dma((nz - 1, 2)),
            dma((nz - 1, 2)),
            dma((nz - 1, 2)),
            dma((nz - 1, 2)),
            dma((2,)),
        ],
        compiler_params=pltpu.CompilerParams(
            collective_id=1, has_side_effects=True, vmem_limit_bytes=40 * 2**20
        ),
        name="exchange",
    )(hidden_in, cotangent, norm_gain.astype(jnp.float32)[:, None], context)

    sign_b = (1 - 2 * column_sign_flips).astype(jnp.float32)[None, :]
    delta = np.arange(row_pad)
    w = segs * delta[None, :] + np.arange(segs)[:, None]
    live = np.broadcast_to(delta[None, :] < deltas, w.shape).reshape(-1)
    w = np.where(live, w.reshape(-1), 0)
    pair_flips = lax.dynamic_slice_in_dim(signs_rows, (pos // 2) * (2 * local_rows), 2 * local_rows, 0)
    flips = pair_flips.reshape(2, deltas, segs).transpose(0, 2, 1)
    flips = jnp.pad(flips, ((0, 0), (0, 0), (0, row_pad - deltas))).reshape(2, 1, -1)
    sign_a = (1 - 2 * flips).astype(jnp.bfloat16)
    ham = hadamard_np(low_rows)[:, w % low_rows]
    member = (np.arange(HALF)[:, None] == (w // low_rows)[None, :]) & live[None, :]
    l = (ham[:, None, :] * member[None, :, :]).reshape(low_rows * HALF, segs * row_pad)
    l = jnp.asarray(l.astype(np.int8)).astype(jnp.bfloat16)[None] * sign_a

    span = min(512, kept // n)
    chunks = kept // span
    own = chunks // n
    partial = pl.pallas_call(
        functools.partial(project_kernel, low_rows, cols, span, row_pad),
        out_shape=jax.ShapeDtypeStruct((n, own, span), jnp.float32),
        in_specs=[smem, smem] + [vmem] * 7,
        out_specs=vmem,
        scratch_shapes=[
            pltpu.VMEM((2, segs * row_pad, cols), jnp.bfloat16),
            pltpu.VMEM((low_rows * cols, 2 * HALF), jnp.float32),
            pltpu.VMEM((span, 2 * HALF), jnp.float32),
        ],
        compiler_params=pltpu.CompilerParams(vmem_limit_bytes=58 * 2**20),
        name="project",
    )(
        (pos // 2 * 2).reshape(1),
        kept_index,
        kept_index.reshape(chunks, span),
        g,
        full_context.reshape(hc, seq),
        sign_b,
        l,
        jnp.asarray(hadamard_np(LOW), jnp.bfloat16),
        jnp.eye(2 * HALF, dtype=jnp.bfloat16),
    )
    scale = 1.0 / math.sqrt(rows_a * cols * seq)
    total = pl.pallas_call(
        functools.partial(scatter_kernel, n, scale),
        out_shape=jax.ShapeDtypeStruct((2, own, span), jnp.float32),
        in_specs=[vmem],
        out_specs=vmem,
        scratch_shapes=[pltpu.VMEM((n - 1, own, span), jnp.float32), dma((n - 1,)), dma((n - 1,))],
        compiler_params=pltpu.CompilerParams(collective_id=0, has_side_effects=True),
        name="scatter_sum",
    )(partial)
    return total.reshape(2, own * span)


def solution(mesh):
    return jax.shard_map(
        functools.partial(on_device, mesh.shape["fsdp"]),
        mesh=mesh,
        in_specs=(
            P(("ckpt", "dp"), "fsdp", None),
            P(("ckpt", "dp"), "fsdp", None),
            P(("ckpt", "dp"), "fsdp", None),
            P("fsdp"),
            P(),
            P(),
            P(),
        ),
        out_specs=P(("ckpt", "dp"), "fsdp"),
        check_vma=False,
    )
```

time: 235 us -> 172 us (0.73)
  waiting for transfers between devices: 96.2 us -> 0 us
  Pallas kernels: 61.1 us -> 157 us
  blocking collectives: 39.9 us -> 0 us
  between operations: 13.4 us -> 0.07 us
  other arithmetic: 12.5 us -> 4.21 us
    pallas_call x0 -> x1, Pallas kernels: none -> 96 us  [on_device(): pl.pallas_call(functools.partial(exchange_kernel, n, d_total, row_pad), o...]
    all_gather x1 -> x0, waiting for transfers between devices: 95.5 us -> none  [on_device(): full_context = lax.all_gather(context, 'fsdp', axis=1, tiled=True)]
    psum x1 -> x0, blocking collectives: 39.9 us -> none  [on_device(): lax.psum((jnp.sum(hidden * hidden, axis=1), jnp.sum(weighted * hidden, ax...]
    reshape x4 -> x0, local copies, waits for them, and re-layouts: 10.2 us -> none  [the longest x2 7.27 us: on_device(): g = grad_hidden.reshape(examples, deltas, parts, seq).transpose(0, 2, 1, 3)]
    unnamed x6 -> x13, local copies, waits for them, and re-layouts: 0.02 us -> 7.68 us
    convert_element_type x2 -> x0, other arithmetic: 5.07 us -> none  [the longest x1 4.39 us: on_device(): grad_hidden = (weighted * inverse[:, None, :] - hidden * (cross_sum * inv...]
    reduce_sum x1 -> x0, other arithmetic: 3.96 us -> none  [on_device(): jnp.sum(hidden * hidden, axis=1)]
  transfers between devices with their start and end apart: 1 -> 0, of which waited for: 1 -> 0; matrix products, arithmetic and copies ran while one was open for 9% -> 0% of each run, Pallas kernels for 0% -> 0%
where the time goes in v2:
time: 172 us; the launch traced here: 171 us
  Pallas kernels  157 us (91%)
  local copies, waits for them, and re-layouts  10.4 us (6%)
  other arithmetic  4.21 us (2%)
    pallas_call x1, Pallas kernels, on_device(): pl.pallas_call(functools.partial(exchange_kernel, n, d_total, row_pad), o...  96 us
    pallas_call x1, Pallas kernels, on_device(): pl.pallas_call(functools.partial(project_kernel, low_rows, cols, span, ro...  52.6 us
    pallas_call x1, Pallas kernels, on_device(): pl.pallas_call(functools.partial(scatter_kernel, n, scale), out_shape=jax...  7.94 us
    unnamed x13, local copies, waits for them, and re-layouts  7.68 us

profile of v2, /device:TPU:0, one launch (start us, length us, event | category | flops | bytes accessed | tf_op | source)
XLA Modules:
  0.0 171.2 jit_solution(4912893379933273761)
XLA Ops:
  0.0 1.5 reshape.37.kept_rows_ref
  1.5 0.8 reshape.41.gain_ref
  2.3 0.0 copy-start
  2.3 1.7 %copy-done = bf16[2,640,1024]{2,1,0:T(8,128)(2,1)S(1)} copy-done((bf16[2,640,1024]{2,1,0:T(8,128)(2,1)S(1)}, bf16[2,640,1024]{2,1,0:T(8,128)(2,1)}, u32[]{:S(2)}) %copy-start) | copy-done | bytes 2621464
  4.0 0.0 copy-start.1
  4.0 1.7 %copy-done.1 = bf16[2,640,1024]{2,1,0:T(8,128)(2,1)S(1)} copy-done((bf16[2,640,1024]{2,1,0:T(8,128)(2,1)S(1)}, bf16[2,640,1024]{2,1,0:T(8,128)(2,1)}, u32[]{:S(2)}) %copy-start.1) | copy-done | bytes 2621464
  5.8 0.0 copy-start.3
  5.8 1.3 copy-done.3
  7.1 0.0 copy-start.5
  7.1 96.0 %exchange.1 = (bf16[4,2,320,1024]{3,2,1,0:T(8,128)(2,1)}, bf16[2,640,1024]{2,1,0:T(8,128)(2,1)S(1)}) custom-call(bf16[2,640,1024]{2,1,0:T(8,128)(2,1)S(1)} %copy-done, bf16[2,640,1024]{2,1,0:T(8,128)(2,1)S(1)} %copy-done.1, f32[640,1]{1,0:T(8,128)S(1)} %reshape.41.gain_ref, bf16[2,320,1024]{2,1,0:T(8,128)(2,1)S(1)} %copy-done.3), custom_call_target="tpu_custom_call" | custom-call | tf_op jit(solution)/shard_map/exchange/pallas_call | solution.py:310
  103.1 0.0 copy-start.2
  103.1 1.5 copy-done.2
  104.7 0.0 copy-done.5
  104.7 0.6 subtract_convert_fusion.1
  105.3 0.8 subtract_convert_fusion
  106.0 0.2 sub.32
  106.3 0.1 copy.11
  106.4 0.1 convert_element_type.25
  106.5 0.0 copy-done.4
  106.5 2.2 %broadcast_multiply_fusion.l_ref = bf16[2,1024,800]{2,1,0:T(8,128)(2,1)} fusion(bf16[2,800]{1,0:T(2,128)(2,1)S(1)} %convert_element_type.25, bf16[1024,800]{1,0:T(8,128)(2,1)S(1)} %copy-done.4), kind=kLoop, calls=%fused_computation | loop fusion | flops 1638400 | bytes 4918400 | tf_op jit(solution)/shard_map/mul | solution.py:352
  108.7 0.6 fusion.eye_ref
  109.3 52.6 %project.1.in_ref = f32[8,4,512]{2,1,0:T(4,128)} custom-call(s32[1]{0:T(128)} %bitcast.pos_ref, s32[16384]{0:T(1024)} %kept_ref.1, s32[32,512]{1,0:T(8,128)} %reshape.37.kept_rows_ref, bf16[2,640,1024]{2,1,0:T(8,128)(2,1)} %copy-done.2, bf16[2560,1024]{1,0:T(8,128)(2,1)} %bitcast.6, f32[1,2048]{1,0:T(1,128)} %bitcast.9, ...), custom_call_target="tpu_custom_call" | custom-call | tf_op jit(solution)/shard_map/project/pallas_call | solution.py:357
  161.9 7.9 %scatter_sum.1 = f32[2,4,512]{2,1,0:T(4,128)} custom-call(f32[8,4,512]{2,1,0:T(4,128)} %project.1.in_ref), custom_call_target="tpu_custom_call" | custom-call | tf_op jit(solution)/shard_map/scatter_sum/pallas_call | solution.py:381
  169.9 1.3 copy.12
  (1 shorter events, 0.0 us)
Async XLA Ops:
  2.3 1.7 %copy-start = (bf16[2,640,1024]{2,1,0:T(8,128)(2,1)S(1)}, bf16[2,640,1024]{2,1,0:T(8,128)(2,1)}, u32[]{:S(2)}) copy-start(bf16[2,640,1024]{2,1,0:T(8,128)(2,1)} %hidden_ref.1) | copy-start | bytes 7864324
  4.0 1.7 %copy-start.1 = (bf16[2,640,1024]{2,1,0:T(8,128)(2,1)S(1)}, bf16[2,640,1024]{2,1,0:T(8,128)(2,1)}, u32[]{:S(2)}) copy-start(bf16[2,640,1024]{2,1,0:T(8,128)(2,1)} %cot_ref.1) | copy-start | bytes 7864324
  5.8 1.3 copy-start.3
  7.1 97.6 %copy-start.5 = (s32[2048]{0:T(1024)S(1)}, s32[2048]{0:T(1024)}, u32[]{:S(2)}) copy-start(s32[2048]{0:T(1024)} %param.14) | copy-start | bytes 24580
  7.1 99.4 %copy-start.4 = (bf16[1024,800]{1,0:T(8,128)(2,1)S(1)}, bf16[1024,800]{1,0:T(8,128)(2,1)}, u32[]{:S(2)}) copy-start(bf16[1024,800]{1,0:T(8,128)(2,1)} %constant.41) | copy-start | bytes 4915204
  103.1 1.6 copy-start.2

commit v3 on v2

--- a/solution.py
+++ b/solution.py
@@ -35,8 +35,8 @@
 
 
 def project_kernel(
-    low_rows, cols, span, row_pad, pos_ref, kept_ref, kept_rows_ref, g_ref, c_ref, b_ref, l_ref, h_ref, eye_ref,
-    out_ref, x_ref, table_ref, buf_ref,
+    low_rows, cols, span, row_pad, pos_ref, kept_ref, kept_rows_ref, g_ref, c_ref, b_ref, a_ref, l_ref, h_ref, eye_ref,
+    out_ref, x_ref, table_ref, even_ref, odd_ref,
 ):
     segs = c_ref.shape[0] // SEG
     parts = cols // SEG
@@ -56,7 +56,8 @@
         start = pl.multiple_of(step * (per_step * HALF), per_step * HALF)
         mixed = []
         for e in range(2):
-            t = jnp.dot(l_ref[e, pl.ds(start, per_step * HALF), :], x_ref[e], preferred_element_type=jnp.float32)
+            left = l_ref[pl.ds(start, per_step * HALF), :] * a_ref[e]
+            t = jnp.dot(left, x_ref[e], preferred_element_type=jnp.float32)
             blocks = [t[:, h * LOW : (h + 1) * LOW] for h in range(high)]
             width = 1
             while width < high:
@@ -83,17 +84,16 @@
     shift = (low_rows * cols).bit_length() - 1
     mask = low_rows * cols - 1
     first_group = pos_ref[0] * GROUPS
-    unroll = 32
-
-    def pick_step(chunk, carry):
-        def rows(group, inner):
-            base = pl.multiple_of(group * unroll, unroll)
-            for u in range(unroll):
-                index = kept_ref[chunk * span + base + u] & mask
-                buf_ref[pl.ds(base + u, 1), :] = table_ref[pl.ds(index, 1), :]
-            return inner
-
-        lax.fori_loop(0, span // unroll, rows, 0)
+    own = out_ref.shape[1]
+    chunks = kept_rows_ref.shape[0]
+
+    def pick(chunk, buf_ref):
+        base = pl.multiple_of(chunk * span, span)
+        for u in range(span):
+            index = kept_ref[base + u] & mask
+            buf_ref[u : u + 1, :] = table_ref[pl.ds(index, 1), :]
+
+    def sign_sum(chunk, buf_ref):
         values = buf_ref[...]
         upper = values.astype(jnp.bfloat16)
         lower = (values - upper.astype(jnp.float32)).astype(jnp.bfloat16)
@@ -102,11 +102,19 @@
         lane = lax.broadcasted_iota(jnp.int32, (2 * HALF, span), 0)
         group_index = first_group + jnp.where(lane >= HALF, lane + (GROUPS - HALF), lane)
         sign = (1 - 2 * parity(group_index & kept_high)).astype(jnp.float32)
-        own = out_ref.shape[1]
         out_ref[chunk // own, pl.ds(lax.rem(chunk, own), 1), :] = jnp.sum(turned * sign, axis=0, keepdims=True)
+
+    odd_ref[...] = jnp.zeros_like(odd_ref)
+
+    def pick_step(step, carry):
+        pick(2 * step, even_ref)
+        sign_sum(lax.max(2 * step - 1, 0), odd_ref)
+        pick(2 * step + 1, odd_ref)
+        sign_sum(2 * step, even_ref)
         return carry
 
-    lax.fori_loop(0, kept_rows_ref.shape[0], pick_step, 0)
+    lax.fori_loop(0, chunks // 2, pick_step, 0)
+    sign_sum(chunks - 1, odd_ref)
 
 
 def greet(n, me):
@@ -130,8 +138,8 @@
 
 
 def exchange_kernel(
-    n, d_total, row_pad, hidden_ref, cot_ref, gain_ref, context_ref, c_ref, g_ref,
-    stats_ref, whole_ref, land_ref, stage_ref, gbuf_ref,
+    n, d_total, row_pad, hidden_in_ref, cot_in_ref, gain_ref, context_ref, c_ref, g_ref,
+    hidden_ref, cot_ref, stats_ref, whole_ref, land_ref, stage_ref, gbuf_ref,
     stat_send, stat_recv, pair_send, pair_recv, right_send, right_recv, left_send, left_recv, local_sem,
 ):
     me = lax.axis_index("fsdp")
@@ -141,6 +149,12 @@
     partner = me + 1 - 2 * y
     local_d, seq = hidden_ref.shape[1:]
     parts = gbuf_ref.shape[1] // row_pad
+    reads = [
+        pltpu.make_async_copy(hidden_in_ref, hidden_ref, local_sem.at[2]),
+        pltpu.make_async_copy(cot_in_ref, cot_ref, local_sem.at[3]),
+    ]
+    for read in reads:
+        read.start()
     greet(n, me)
 
     def right(step, sub):
@@ -179,6 +193,8 @@
     start_both(0, 0)
     keep = pltpu.make_async_copy(context_ref.at[y], c_ref.at[z, y], local_sem.at[0])
     keep.start()
+    for read in reads:
+        read.wait()
 
     rows = 32
 
@@ -313,9 +329,11 @@
             jax.ShapeDtypeStruct((nz, 2, local_hc, seq), jnp.bfloat16),
             jax.ShapeDtypeStruct((2, parts * row_pad, seq), jnp.bfloat16),
         ),
-        in_specs=[vmem, vmem, vmem, anywhere],
+        in_specs=[anywhere, anywhere, vmem, anywhere],
         out_specs=(anywhere, anywhere),
         scratch_shapes=[
+            pltpu.VMEM(hidden_in.shape, jnp.bfloat16),
+            pltpu.VMEM(hidden_in.shape, jnp.bfloat16),
             pltpu.VMEM((8, seq), jnp.float32),
             pltpu.VMEM((4, 1, seq), jnp.float32),
             pltpu.VMEM((n, 8, seq), jnp.float32),
@@ -329,10 +347,10 @@
             dma((nz - 1, 2)),
             dma((nz - 1, 2)),
             dma((nz - 1, 2)),
-            dma((2,)),
+            dma((4,)),
         ],
         compiler_params=pltpu.CompilerParams(
-            collective_id=1, has_side_effects=True, vmem_limit_bytes=40 * 2**20
+            collective_id=1, has_side_effects=True, vmem_limit_bytes=60 * 2**20
         ),
         name="exchange",
     )(hidden_in, cotangent, norm_gain.astype(jnp.float32)[:, None], context)
@@ -349,7 +367,7 @@
     ham = hadamard_np(low_rows)[:, w % low_rows]
     member = (np.arange(HALF)[:, None] == (w // low_rows)[None, :]) & live[None, :]
     l = (ham[:, None, :] * member[None, :, :]).reshape(low_rows * HALF, segs * row_pad)
-    l = jnp.asarray(l.astype(np.int8)).astype(jnp.bfloat16)[None] * sign_a
+    l = jnp.asarray(l, jnp.bfloat16)
 
     span = min(512, kept // n)
     chunks = kept // span
@@ -357,11 +375,12 @@
     partial = pl.pallas_call(
         functools.partial(project_kernel, low_rows, cols, span, row_pad),
         out_shape=jax.ShapeDtypeStruct((n, own, span), jnp.float32),
-        in_specs=[smem, smem] + [vmem] * 7,
+        in_specs=[smem, smem] + [vmem] * 8,
         out_specs=vmem,
         scratch_shapes=[
             pltpu.VMEM((2, segs * row_pad, cols), jnp.bfloat16),
             pltpu.VMEM((low_rows * cols, 2 * HALF), jnp.float32),
+            pltpu.VMEM((span, 2 * HALF), jnp.float32),
             pltpu.VMEM((span, 2 * HALF), jnp.float32),
         ],
         compiler_params=pltpu.CompilerParams(vmem_limit_bytes=58 * 2**20),
@@ -373,6 +392,7 @@
         g,
         full_context.reshape(hc, seq),
         sign_b,
+        sign_a,
         l,
         jnp.asarray(hadamard_np(LOW), jnp.bfloat16),
         jnp.eye(2 * HALF, dtype=jnp.bfloat16),

time: 172 us -> 160 us (0.930)
  local copies, waits for them, and re-layouts: 10.4 us -> 4.57 us
  Pallas kernels: 157 us -> 153 us
  other arithmetic: 4.21 us -> 2.01 us
    unnamed x13 -> x5, local copies, waits for them, and re-layouts: 7.68 us -> 1.34 us
    pallas_call x1, Pallas kernels: 52.6 us -> 47.4 us  [on_device(): pl.pallas_call(functools.partial(project_kernel, low_rows, cols, span, ro...]
    mul x1 -> x0, other arithmetic: 2.2 us -> none  [on_device(): l = jnp.asarray(l.astype(np.int8)).astype(jnp.bfloat16)[None] * sign_a]
where the time goes in v3:
time: 160 us; the launch traced here: 159 us
  Pallas kernels  153 us (96%)
  local copies, waits for them, and re-layouts  4.57 us (3%)
  other arithmetic  2.01 us (1%)
    pallas_call x1, Pallas kernels, on_device(): pl.pallas_call(functools.partial(exchange_kernel, n, d_total, row_pad), o...  97.2 us
    pallas_call x1, Pallas kernels, on_device(): pl.pallas_call(functools.partial(project_kernel, low_rows, cols, span, ro...  47.4 us
    pallas_call x1, Pallas kernels, on_device(): pl.pallas_call(functools.partial(scatter_kernel, n, scale), out_shape=jax...  7.94 us

profile of v3, /device:TPU:0, one launch (start us, length us, event | category | flops | bytes accessed | tf_op | source)
XLA Modules:
  0.0 159.2 jit_solution(1782952377249610054)
XLA Ops:
  0.0 0.8 subtract_convert_fusion
  0.8 0.2 sub.35
  1.0 0.1 copy.11
  1.1 0.7 convert_element_type.16.a_ref
  1.8 1.6 reshape.49.gain_ref
  3.4 0.0 copy-start
  3.4 0.0 copy-start.1
  3.4 97.2 %exchange.1 = (bf16[4,2,320,1024]{3,2,1,0:T(8,128)(2,1)}, bf16[2,640,1024]{2,1,0:T(8,128)(2,1)}) custom-call(bf16[2,640,1024]{2,1,0:T(8,128)(2,1)} %hidden_in_ref.1, bf16[2,640,1024]{2,1,0:T(8,128)(2,1)} %cot_in_ref.1, f32[640,1]{1,0:T(8,128)} %reshape.49.gain_ref, bf16[2,320,1024]{2,1,0:T(8,128)(2,1)} %context_ref.1), custom_call_target="tpu_custom_call" | custom-call | tf_op jit(solution)/shard_map/exchange/pallas_call | solution.py:326
  100.6 0.0 copy-done
  100.6 0.6 reshape.45.kept_rows_ref
  101.3 0.6 fusion.eye_ref
  101.9 0.0 copy-done.1
  101.9 0.6 subtract_convert_fusion.1
  102.5 47.4 %project.1.in_ref = f32[8,4,512]{2,1,0:T(4,128)} custom-call(s32[1]{0:T(128)} %bitcast.pos_ref, s32[16384]{0:T(1024)} %kept_ref.1, s32[32,512]{1,0:T(8,128)} %reshape.45.kept_rows_ref, bf16[2,640,1024]{2,1,0:T(8,128)(2,1)} %get-tuple-element.7.g_ref, bf16[2560,1024]{1,0:T(8,128)(2,1)} %bitcast.6, f32[1,2048]{1,0:T(1,128)} %bitcast.9, ...), custom_call_target="tpu_custom_call" | custom-call | tf_op jit(solution)/shard_map/project/pallas_call | solution.py:375
  149.9 7.9 %scatter_sum.1 = f32[2,4,512]{2,1,0:T(4,128)} custom-call(f32[8,4,512]{2,1,0:T(4,128)} %project.1.in_ref), custom_call_target="tpu_custom_call" | custom-call | tf_op jit(solution)/shard_map/scatter_sum/pallas_call | solution.py:401
  157.9 1.3 copy.13
Async XLA Ops:
  3.4 97.3 %copy-start = (s32[16384]{0:T(1024)S(1)}, s32[16384]{0:T(1024)}, u32[]{:S(2)}) copy-start(s32[16384]{0:T(1024)} %kept_ref.1) | copy-start | bytes 196612
  3.4 98.5 %copy-start.1 = (s32[2048]{0:T(1024)S(1)}, s32[2048]{0:T(1024)}, u32[]{:S(2)}) copy-start(s32[2048]{0:T(1024)} %param.14) | copy-start | bytes 24580

commit v4 on v3

--- a/solution.py
+++ b/solution.py
@@ -35,20 +35,30 @@
 
 
 def project_kernel(
-    low_rows, cols, span, row_pad, pos_ref, kept_ref, kept_rows_ref, g_ref, c_ref, b_ref, a_ref, l_ref, h_ref, eye_ref,
-    out_ref, x_ref, table_ref, even_ref, odd_ref,
+    low_rows, cols, span, row_pad, pos_ref, kept_ref, kept_rows_ref, g_ref, c_in_ref, b_ref, a_ref, l_in_ref, h_ref, eye_ref,
+    out_ref, x_ref, table_ref, even_ref, odd_ref, c_ref, l_ref, sem,
 ):
-    segs = c_ref.shape[0] // SEG
+    segs = c_in_ref.shape[0] // SEG
     parts = cols // SEG
-    for e in range(2):
-        for nb in range(segs):
+    loads = [
+        pltpu.make_async_copy(c_in_ref.at[pl.ds(nb * SEG, SEG)], c_ref.at[pl.ds(nb * SEG, SEG)], sem.at[nb])
+        for nb in range(segs)
+    ]
+    loads.append(pltpu.make_async_copy(l_in_ref, l_ref, sem.at[segs]))
+    for load in loads:
+        load.start()
+    sign_b = (1 - 2 * b_ref[...]).astype(jnp.float32)
+    for nb in range(segs):
+        loads[nb].wait()
+        for e in range(2):
             block = dot_nt(g_ref[e], c_ref[nb * SEG : (nb + 1) * SEG, :])
             for gamma in range(parts):
                 omega, sigma = divmod(segs * gamma + nb, parts)
-                signed = block[gamma * row_pad : (gamma + 1) * row_pad] * b_ref[0:1, sigma * SEG : (sigma + 1) * SEG]
+                signed = block[gamma * row_pad : (gamma + 1) * row_pad] * sign_b[:, sigma * SEG : (sigma + 1) * SEG]
                 x_ref[e, omega * row_pad : (omega + 1) * row_pad, sigma * SEG : (sigma + 1) * SEG] = signed.astype(
                     jnp.bfloat16
                 )
+    loads[segs].wait()
     per_step = min(low_rows, 4)
     high = cols // LOW
 
@@ -253,9 +263,7 @@
     gradient_of(1 - y, 0)
     give = remote(gbuf_ref.at[0], g_ref.at[y], pair_send.at[1], pair_recv.at[1], partner)
     give.start()
-    gradient_of(y, 1)
     hold = pltpu.make_async_copy(gbuf_ref.at[1], g_ref.at[y], local_sem.at[1])
-    hold.start()
 
     for step in range(nz - 1):
         for sub in range(2):
@@ -269,6 +277,9 @@
 
             if step + 1 < nz - 1:
                 start_both(step + 1, sub)
+            if step == 0 and sub == 0:
+                gradient_of(y, 1)
+                hold.start()
     for step in range(nz - 1):
         for sub in range(2):
 
@@ -355,7 +366,6 @@
         name="exchange",
     )(hidden_in, cotangent, norm_gain.astype(jnp.float32)[:, None], context)
 
-    sign_b = (1 - 2 * column_sign_flips).astype(jnp.float32)[None, :]
     delta = np.arange(row_pad)
     w = segs * delta[None, :] + np.arange(segs)[:, None]
     live = np.broadcast_to(delta[None, :] < deltas, w.shape).reshape(-1)
@@ -375,13 +385,16 @@
     partial = pl.pallas_call(
         functools.partial(project_kernel, low_rows, cols, span, row_pad),
         out_shape=jax.ShapeDtypeStruct((n, own, span), jnp.float32),
-        in_specs=[smem, smem] + [vmem] * 8,
+        in_specs=[smem, smem, vmem, vmem, anywhere, vmem, vmem, anywhere, vmem, vmem],
         out_specs=vmem,
         scratch_shapes=[
             pltpu.VMEM((2, segs * row_pad, cols), jnp.bfloat16),
             pltpu.VMEM((low_rows * cols, 2 * HALF), jnp.float32),
             pltpu.VMEM((span, 2 * HALF), jnp.float32),
             pltpu.VMEM((span, 2 * HALF), jnp.float32),
+            pltpu.VMEM((hc, seq), jnp.bfloat16),
+            pltpu.VMEM(l.shape, jnp.bfloat16),
+            dma((segs + 1,)),
         ],
         compiler_params=pltpu.CompilerParams(vmem_limit_bytes=58 * 2**20),
         name="project",
@@ -391,11 +404,11 @@
         kept_index.reshape(chunks, span),
         g,
         full_context.reshape(hc, seq),
-        sign_b,
+        column_sign_flips[None, :],
         sign_a,
         l,
         jnp.asarray(hadamard_np(LOW), jnp.bfloat16),
-        jnp.eye(2 * HALF, dtype=jnp.bfloat16),
+        jnp.asarray(np.eye(2 * HALF), jnp.bfloat16),
     )
     scale = 1.0 / math.sqrt(rows_a * cols * seq)
     total = pl.pallas_call(

time: 160 us -> 158 us (0.988)
  no operation moved by 1% of the time
where the time goes in v4:
time: 158 us
  Pallas kernels  153 us (97%)
  local copies, waits for them, and re-layouts  4.55 us (3%)
    pallas_call x1, Pallas kernels, on_device(): pl.pallas_call(functools.partial(exchange_kernel, n, d_total, row_pad), o...  97.2 us
    pallas_call x1, Pallas kernels, on_device(): pl.pallas_call(functools.partial(project_kernel, low_rows, cols, span, ro...  47.4 us
    pallas_call x1, Pallas kernels, on_device(): pl.pallas_call(functools.partial(scatter_kernel, n, scale), out_shape=jax...  7.96 us

profile of v4, /device:TPU:0, one launch (start us, length us, event | category | flops | bytes accessed | tf_op | source)
XLA Modules:
  0.0 158.0 jit_solution(1177822024819156027)
XLA Ops:
  0.0 0.8 subtract_convert_fusion
  0.8 0.2 sub.27
  1.0 0.1 copy.12
  1.1 0.7 convert_element_type.8.a_ref
  1.8 1.6 reshape.49.gain_ref
  3.4 0.0 copy-start
  3.4 97.2 %exchange.1 = (bf16[4,2,320,1024]{3,2,1,0:T(8,128)(2,1)}, bf16[2,640,1024]{2,1,0:T(8,128)(2,1)}) custom-call(bf16[2,640,1024]{2,1,0:T(8,128)(2,1)} %hidden_in_ref.1, bf16[2,640,1024]{2,1,0:T(8,128)(2,1)} %cot_in_ref.1, f32[640,1]{1,0:T(8,128)} %reshape.49.gain_ref, bf16[2,320,1024]{2,1,0:T(8,128)(2,1)} %context_ref.1), custom_call_target="tpu_custom_call" | custom-call | tf_op jit(solution)/shard_map/exchange/pallas_call | solution.py:337
  100.6 0.0 copy-done
  100.6 0.6 reshape.45.kept_rows_ref
  101.3 47.4 %project.1.in_ref = f32[8,4,512]{2,1,0:T(4,128)} custom-call(s32[1]{0:T(128)} %bitcast.pos_ref, s32[16384]{0:T(1024)} %kept_ref.1, s32[32,512]{1,0:T(8,128)} %reshape.45.kept_rows_ref, bf16[2,640,1024]{2,1,0:T(8,128)(2,1)} %get-tuple-element.7.g_ref, bf16[2560,1024]{1,0:T(8,128)(2,1)} %bitcast.6, s32[1,2048]{1,0:T(1,128)} %bitcast.9, ...), custom_call_target="tpu_custom_call" | custom-call | tf_op jit(solution)/shard_map/project/pallas_call | solution.py:385
  148.7 8.0 %scatter_sum.1 = f32[2,4,512]{2,1,0:T(4,128)} custom-call(f32[8,4,512]{2,1,0:T(4,128)} %project.1.in_ref), custom_call_target="tpu_custom_call" | custom-call | tf_op jit(solution)/shard_map/scatter_sum/pallas_call | solution.py:414
  156.7 1.3 copy.14
Async XLA Ops:
  3.4 97.3 %copy-start = (s32[16384]{0:T(1024)S(1)}, s32[16384]{0:T(1024)}, u32[]{:S(2)}) copy-start(s32[16384]{0:T(1024)} %kept_ref.1) | copy-start | bytes 196612

commit v5 on v4

--- a/solution.py
+++ b/solution.py
@@ -92,7 +92,6 @@
     lax.fori_loop(0, low_rows // per_step, table_step, 0)
 
     shift = (low_rows * cols).bit_length() - 1
-    mask = low_rows * cols - 1
     first_group = pos_ref[0] * GROUPS
     own = out_ref.shape[1]
     chunks = kept_rows_ref.shape[0]
@@ -100,7 +99,7 @@
     def pick(chunk, buf_ref):
         base = pl.multiple_of(chunk * span, span)
         for u in range(span):
-            index = kept_ref[base + u] & mask
+            index = kept_ref[base + u]
             buf_ref[u : u + 1, :] = table_ref[pl.ds(index, 1), :]
 
     def sign_sum(chunk, buf_ref):
@@ -400,7 +399,7 @@
         name="project",
     )(
         (pos // 2 * 2).reshape(1),
-        kept_index,
+        kept_index & (low_rows * cols - 1),
         kept_index.reshape(chunks, span),
         g,
         full_context.reshape(hc, seq),

time: 158 us -> 155 us (0.981)
  Pallas kernels: 153 us -> 149 us
    pallas_call x1, Pallas kernels: 47.4 us -> 43.9 us  [on_device(): pl.pallas_call(functools.partial(project_kernel, low_rows, cols, span, ro...]
where the time goes in v5:
time: 155 us
  Pallas kernels  149 us (96%)
  local copies, waits for them, and re-layouts  4.55 us (3%)
    pallas_call x1, Pallas kernels, on_device(): pl.pallas_call(functools.partial(exchange_kernel, n, d_total, row_pad), o...  97.2 us
    pallas_call x1, Pallas kernels, on_device(): pl.pallas_call(functools.partial(project_kernel, low_rows, cols, span, ro...  43.9 us
    pallas_call x1, Pallas kernels, on_device(): pl.pallas_call(functools.partial(scatter_kernel, n, scale), out_shape=jax...  7.96 us

profile of v5, /device:TPU:0, one launch (start us, length us, event | category | flops | bytes accessed | tf_op | source)
XLA Modules:
  0.0 155.1 jit_solution(5531660725866610546)
XLA Ops:
  0.0 0.8 subtract_convert_fusion
  0.8 0.2 sub.27
  1.0 0.1 copy.12
  1.1 0.7 convert_element_type.8.a_ref
  1.8 1.6 %reshape.49.gain_ref = f32[640,1]{1,0:T(8,128)} reshape(bf16[640]{0:T(1024)(128)(2,1)} %param.13) | data formatting | bytes 3840 | tf_op jit(solution)/shard_map/broadcast_in_dim | solution.py:366
  3.4 0.0 copy-start
  3.4 97.2 %exchange.1 = (bf16[4,2,320,1024]{3,2,1,0:T(8,128)(2,1)}, bf16[2,640,1024]{2,1,0:T(8,128)(2,1)}) custom-call(bf16[2,640,1024]{2,1,0:T(8,128)(2,1)} %hidden_in_ref.1, bf16[2,640,1024]{2,1,0:T(8,128)(2,1)} %cot_in_ref.1, f32[640,1]{1,0:T(8,128)} %reshape.49.gain_ref, bf16[2,320,1024]{2,1,0:T(8,128)(2,1)} %context_ref.1), custom_call_target="tpu_custom_call" | custom-call | tf_op jit(solution)/shard_map/exchange/pallas_call | solution.py:336
  100.6 0.0 copy-done
  100.6 0.6 broadcast_and_fusion.kept_ref
  101.3 0.6 reshape.45.kept_rows_ref
  101.9 43.9 %project.1.in_ref = f32[8,4,512]{2,1,0:T(4,128)} custom-call(s32[1]{0:T(128)} %bitcast.pos_ref, s32[16384]{0:T(1024)} %broadcast_and_fusion.kept_ref, s32[32,512]{1,0:T(8,128)} %reshape.45.kept_rows_ref, bf16[2,640,1024]{2,1,0:T(8,128)(2,1)} %get-tuple-element.7.g_ref, bf16[2560,1024]{1,0:T(8,128)(2,1)} %bitcast.6, s32[1,2048]{1,0:T(1,128)} %bitcast.9, ...), custom_call_target="tpu_custom_call" | custom-call | tf_op jit(solution)/shard_map/project/pallas_call | solution.py:384
  145.8 8.0 %scatter_sum.1 = f32[2,4,512]{2,1,0:T(4,128)} custom-call(f32[8,4,512]{2,1,0:T(4,128)} %project.1.in_ref), custom_call_target="tpu_custom_call" | custom-call | tf_op jit(solution)/shard_map/scatter_sum/pallas_call | solution.py:413
  153.8 1.3 copy.14
Async XLA Ops:
  3.4 97.3 %copy-start = (s32[16384]{0:T(1024)S(1)}, s32[16384]{0:T(1024)}, u32[]{:S(2)}) copy-start(s32[16384]{0:T(1024)} %param.16) | copy-start | bytes 196612
